TPU v7x, 512 devices: a whole 4x8x8 slice. The times are simulated.
512 devices in a mesh: src: 16 (over x, y_hi, core), tgt: 32 (over y_lo, z).
Axes of the slice: x: 4, y: 8 (y_hi: 2, y_lo: 4; y = y_hi * 4 + y_lo), z: 8, core: 2. Of those that a mesh axis runs over, the one named last changes fastest.
Arguments:
- coefficients: bfloat16 [16, 32, 512, 512], P('src', 'tgt'), may hold values from -6 to 6
- transfer_blocks: bfloat16 [4, 16, 32, 512, 1024], P(None, 'src', 'tgt'), may hold values from -0.1875 to 0.1875
Outputs:
- result: bfloat16 [16, 32, 512, 512], P('src', 'tgt')
All inputs are finite; a program needn't handle non-finite values.
Results may differ from a plain program's by a relative error of at most 0.0064.
Values may be sent and summed in bfloat16 or wider, within the bound.
A program may use at most 64 MiB of HBM per device.

v0:
```python
import jax
import jax.numpy as jnp
from jax import lax
from jax.sharding import PartitionSpec as P


def from_partner(value, axis, distance):
    return lax.ppermute(value, axis, [(i, i ^ 1 << distance) for i in range(lax.axis_size(axis))])


def combine(own_part, partner, block_now, upper_half, rank_rows):
    own_cols = lax.dynamic_slice_in_dim(block_now, upper_half * rank_rows, rank_rows, 1)
    other_cols = lax.dynamic_slice_in_dim(block_now, (1 - upper_half) * rank_rows, rank_rows, 1)
    total = jnp.dot(own_cols, own_part, preferred_element_type=jnp.float32)
    total = total + jnp.dot(other_cols, partner, preferred_element_type=jnp.float32)
    return total.astype(jnp.bfloat16)


def shards(coefficients, transfer_blocks):
    rank_rows = coefficients.shape[2]
    columns = coefficients.shape[3]
    current = coefficients[0, 0]
    blocks = transfer_blocks[:, 0, 0]
    src_top = lax.axis_size("src").bit_length() - 2
    tgt_count = lax.axis_size("tgt")
    tgt_top = tgt_count.bit_length() - 2
    src_place = lax.axis_index("src")
    tgt_place = lax.axis_index("tgt")
    partner = from_partner(current, "src", 0)
    current = combine(current, partner, blocks[0], src_place & 1, rank_rows)
    partner = from_partner(current, "src", src_top)
    current = combine(current, partner, blocks[1], src_place >> src_top & 1, rank_rows)
    slab_rows = rank_rows // tgt_count
    pieces = current.reshape(tgt_count, slab_rows, columns)
    mirrored = pieces.reshape(tgt_count >> tgt_top + 1, 2, 1 << tgt_top, slab_rows, columns)
    mirrored = mirrored[:, ::-1].reshape(tgt_count, slab_rows, columns)
    joined = jnp.stack([pieces, mirrored], 1).reshape(2 * rank_rows, columns)
    arrived = lax.all_to_all(joined, "tgt", split_axis=0, concat_axis=0, tiled=True)
    arrived = arrived.reshape(tgt_count, 2, slab_rows, columns)
    current = arrived[:, 0].reshape(rank_rows, columns)
    partner = arrived[:, 1].reshape(rank_rows, columns)
    current = combine(current, partner, blocks[2], tgt_place >> tgt_top & 1, rank_rows)
    partner = from_partner(current, "tgt", 0)
    current = combine(current, partner, blocks[3], tgt_place & 1, rank_rows)
    return current[None, None]


def solution(mesh):
    return jax.shard_map(
        shards,
        mesh=mesh,
        in_specs=(P("src", "tgt", None, None), P(None, "src", "tgt", None, None)),
        out_specs=P("src", "tgt", None, None),
        check_vma=False,
    )
```

profile of v0, /device:TPU:16, one launch (start us, length us, event | category | flops | bytes accessed | tf_op | source)
XLA Modules:
  0.0 86.3 jit_solution(5083811921228645498)
XLA Ops:
  0.0 1.9 %collective-permute-start = (bf16[512,512]{1,0:T(8,128)(2,1)}, bf16[512,512]{1,0:T(8,128)(2,1)}, u32[]{:S(2)}, u32[]{:S(2)}) collective-permute-start(bf16[512,512]{1,0:T(8,128)(2,1)} %bitcast.51), channel_id=1, source_target_pairs={{0,32},{32,0},{64,96},{96,64},{128,160},{160,128},{192,224},{224,1... | collective-permute-start | bytes 1572872 | tf_op jit(solution)/shard_map/ppermute | solution.py:8
  1.9 0.0 copy-start.1
  1.9 2.8 %fusion.34 = (bf16[1,1,1,512,1024]{4,3,2,1,0:T(8,128)(2,1)S(1)}, bf16[1,1,1,512,1024]{4,3,2,1,0:T(8,128)(2,1)S(1)}, bf16[1,1,1,512,1024]{4,3,2,1,0:T(8,128)(2,1)S(1)}, bf16[1,1,1,512,1024]{4,3,2,1,0:T(8,128)(2,1)S(1)}) fusion(bf16[4,1,1,512,1024]{4,3,2,1,0:T(8,128)(2,1)} %param.3), kind=kLoop, calls=%fused_computation.39 | loop fusion | bytes 8388608 | tf_op jit(solution)/shard_map/slice | solution.py:44
  4.7 0.0 copy-start
  4.7 0.0 copy-done.1
  4.7 0.4 fusion.9
  5.2 0.0 collective-permute-done
  5.2 2.3 %fusion = bf16[512,512]{1,0:T(8,128)(2,1)} fusion(f32[512,512]{1,0:T(8,128)S(1)} %fusion.9, bf16[512,512]{1,0:T(8,128)(2,1)} %collective-permute-done, bf16[1,1,1,512,1024]{4,3,2,1,0:T(8,128)(2,1)S(1)} %get-tuple-element.7, s32[]{:T(128)S(6)} %select_n.28), kind=kOutput, calls=%fused_computation.4 | convolution fusion | flops 268959744 | bytes 2621444 | tf_op jit(solution)/shard_map/dot_general | solution.py:15
  7.5 4.9 %collective-permute-start.1 = (bf16[512,512]{1,0:T(8,128)(2,1)}, bf16[512,512]{1,0:T(8,128)(2,1)}, u32[]{:S(2)}, u32[]{:S(2)}) collective-permute-start(bf16[512,512]{1,0:T(8,128)(2,1)} %fusion), channel_id=1, source_target_pairs={{0,256},{32,288},{64,320},{96,352},{128,384},{160,416},{192,448},{... | collective-permute-start | bytes 1572872 | tf_op jit(solution)/shard_map/ppermute | solution.py:8
  12.4 1.5 %fusion.11 = f32[512,512]{1,0:T(8,128)S(1)} fusion(bf16[512,512]{1,0:T(8,128)(2,1)} %fusion, bf16[1,1,1,512,1024]{4,3,2,1,0:T(8,128)(2,1)S(1)} %get-tuple-element.8, s32[]{:T(128)S(6)} %select_n.26), kind=kOutput, calls=%fused_computation.16 | convolution fusion | flops 268435456 | bytes 2097156 | tf_op jit(solution)/shard_map/dot_general | solution.py:14
  13.9 0.0 copy-done
  13.9 11.6 %collective-permute-done.1 = bf16[512,512]{1,0:T(8,128)(2,1)} collective-permute-done((bf16[512,512]{1,0:T(8,128)(2,1)}, bf16[512,512]{1,0:T(8,128)(2,1)}, u32[]{:S(2)}, u32[]{:S(2)}) %collective-permute-start.1) | collective-permute-done | bytes 524320 | tf_op jit(solution)/shard_map/ppermute | solution.py:8
  25.5 1.6 %fusion.1 = bf16[512,512]{1,0:T(8,128)(2,1)S(1)} fusion(f32[512,512]{1,0:T(8,128)S(1)} %fusion.11, bf16[512,512]{1,0:T(8,128)(2,1)} %collective-permute-done.1, bf16[1,1,1,512,1024]{4,3,2,1,0:T(8,128)(2,1)} %copy-done, s32[]{:T(128)S(6)} %select_n.29), kind=kOutput, calls=%fused_computation.5 | convolution fusion | flops 268959744 | bytes 2621444 | tf_op jit(solution)/shard_map/dot_general | solution.py:15
  27.2 1.1 %pad_maximum_fusion = bf16[32,2,16,512]{3,2,1,0:T(8,128)(2,1)} fusion(bf16[32,1,16,512]{3,2,1,0:T(8,128)(2,1)S(1)} %bitcast.49, bf16[32,1,16,512]{3,2,1,0:T(8,128)(2,1)S(1)} %bitcast.46), kind=kLoop, calls=%fused_computation.9 | loop fusion | flops 524288 | bytes 2097152 | tf_op jit(solution)/shard_map/stack | solution.py:37
  28.2 13.8 %all-to-all-start = ((bf16[32,32,512]{2,1,0:T(8,128)(2,1)}), bf16[32,32,512]{2,1,0:T(8,128)(2,1)S(1)}, u32[]{:S(2)}, u32[]{:S(2)}) async-start(bf16[32,32,512]{2,1,0:T(8,128)(2,1)} %bitcast.11), calls=%async_computation | async-start | bytes 2097152 | tf_op jit(solution)/shard_map/all_to_all | solution.py:38
  42.1 27.2 %all-to-all-done = bf16[32,32,512]{2,1,0:T(8,128)(2,1)S(1)} async-done(((bf16[32,32,512]{2,1,0:T(8,128)(2,1)}), bf16[32,32,512]{2,1,0:T(8,128)(2,1)S(1)}, u32[]{:S(2)}, u32[]{:S(2)}) %all-to-all-start) | async-done | bytes 1048608 | tf_op jit(solution)/shard_map/all_to_all | solution.py:38
  69.4 0.1 fusion.35
  69.4 0.4 fusion.13
  69.9 0.4 fusion.2
  70.3 2.5 %collective-permute-start.2 = (bf16[512,512]{1,0:T(8,128)(2,1)S(1)}, bf16[512,512]{1,0:T(8,128)(2,1)S(1)}, u32[]{:S(2)}, u32[]{:S(2)}) collective-permute-start(bf16[512,512]{1,0:T(8,128)(2,1)S(1)} %fusion.2), channel_id=1, source_target_pairs={{0,1},{1,0},{2,3},{3,2},{4,5},{5,4},{6,7},{7,6},{8,9},{9,8},{10,11... | collective-permute-start | bytes 1572872 | tf_op jit(solution)/shard_map/ppermute | solution.py:8
  72.8 0.4 fusion.15
  73.3 11.8 %collective-permute-done.2 = bf16[512,512]{1,0:T(8,128)(2,1)S(1)} collective-permute-done((bf16[512,512]{1,0:T(8,128)(2,1)S(1)}, bf16[512,512]{1,0:T(8,128)(2,1)S(1)}, u32[]{:S(2)}, u32[]{:S(2)}) %collective-permute-start.2) | collective-permute-done | bytes 524320 | tf_op jit(solution)/shard_map/ppermute | solution.py:8
  85.1 1.2 %fusion.4 = bf16[1,1,512,512]{3,2,1,0:T(8,128)(2,1)} fusion(f32[512,512]{1,0:T(8,128)S(1)} %fusion.15, bf16[512,512]{1,0:T(8,128)(2,1)S(1)} %collective-permute-done.2, bf16[1,1,1,512,1024]{4,3,2,1,0:T(8,128)(2,1)S(1)} %get-tuple-element.5, s32[]{:T(128)S(6)} %select_n.31), kind=kOutput, calls=%fused_computation.8 | convolution fusion | flops 268959744 | bytes 2621444 | tf_op jit(solution)/shard_map/dot_general | solution.py:15
  (1 shorter events, 0.0 us)
Async XLA Ops:
  0.0 5.2 %collective-permute-start = (bf16[512,512]{1,0:T(8,128)(2,1)}, bf16[512,512]{1,0:T(8,128)(2,1)}, u32[]{:S(2)}, u32[]{:S(2)}) collective-permute-start(bf16[512,512]{1,0:T(8,128)(2,1)} %bitcast.51), channel_id=1, source_target_pairs={{0,32},{32,0},{64,96},{96,64},{128,160},{160,128},{192,224},{224,1... | collective-permute-start | bytes 1572872 | tf_op jit(solution)/shard_map/ppermute | solution.py:8
  1.9 2.8 %copy-start.1 = (bf16[1,1,512,512]{3,2,1,0:T(8,128)(2,1)S(1)}, bf16[1,1,512,512]{3,2,1,0:T(8,128)(2,1)}, u32[]{:S(2)}) copy-start(bf16[1,1,512,512]{3,2,1,0:T(8,128)(2,1)} %param.2) | copy-start | bytes 1572868
  4.7 9.2 %copy-start = (bf16[1,1,1,512,1024]{4,3,2,1,0:T(8,128)(2,1)}, bf16[1,1,1,512,1024]{4,3,2,1,0:T(8,128)(2,1)S(1)}, u32[]{:S(2)}) copy-start(bf16[1,1,1,512,1024]{4,3,2,1,0:T(8,128)(2,1)S(1)} %get-tuple-element.8) | copy-start | bytes 3145732
  7.5 18.0 %collective-permute-start.1 = (bf16[512,512]{1,0:T(8,128)(2,1)}, bf16[512,512]{1,0:T(8,128)(2,1)}, u32[]{:S(2)}, u32[]{:S(2)}) collective-permute-start(bf16[512,512]{1,0:T(8,128)(2,1)} %fusion), channel_id=1, source_target_pairs={{0,256},{32,288},{64,320},{96,352},{128,384},{160,416},{192,448},{... | collective-permute-start | bytes 1572872 | tf_op jit(solution)/shard_map/ppermute | solution.py:8
  28.2 41.1 %all-to-all-start = ((bf16[32,32,512]{2,1,0:T(8,128)(2,1)}), bf16[32,32,512]{2,1,0:T(8,128)(2,1)S(1)}, u32[]{:S(2)}, u32[]{:S(2)}) async-start(bf16[32,32,512]{2,1,0:T(8,128)(2,1)} %bitcast.11), calls=%async_computation | async-start | bytes 2097152 | tf_op jit(solution)/shard_map/all_to_all | solution.py:38
  70.3 14.7 %collective-permute-start.2 = (bf16[512,512]{1,0:T(8,128)(2,1)S(1)}, bf16[512,512]{1,0:T(8,128)(2,1)S(1)}, u32[]{:S(2)}, u32[]{:S(2)}) collective-permute-start(bf16[512,512]{1,0:T(8,128)(2,1)S(1)} %fusion.2), channel_id=1, source_target_pairs={{0,1},{1,0},{2,3},{3,2},{4,5},{5,4},{6,7},{7,6},{8,9},{9,8},{10,11... | collective-permute-start | bytes 1572872 | tf_op jit(solution)/shard_map/ppermute | solution.py:8
where the time goes:
time: 86.7 us; the launch traced here: 86.3 us
  waiting for transfers between devices  50.6 us (58%)
  starting transfers between devices  23.2 us (27%)
  matrix products  8.38 us (10%)
  local copies, waits for them, and re-layouts  2.89 us (3%)
  other arithmetic  1.06 us (1%)
    all_to_all x1, waiting for transfers between devices, shards(): lax.all_to_all(joined, 'tgt', split_axis=0, concat_axis=0, tiled=True)  27.2 us
    ppermute x3, waiting for transfers between devices, from_partner(): lax.ppermute(value, axis, [(i, i ^ 1 << distance) for i in range(lax.axis...  23.4 us
    all_to_all x1, starting transfers between devices, shards(): lax.all_to_all(joined, 'tgt', split_axis=0, concat_axis=0, tiled=True)  13.8 us
    ppermute x3, starting transfers between devices, from_partner(): lax.ppermute(value, axis, [(i, i ^ 1 << distance) for i in range(lax.axis...  9.34 us
    dot_general x4, matrix products, combine(): jnp.dot(other_cols, partner, preferred_element_type=jnp.float32)  5.59 us
    dot_general x4, matrix products, combine(): total = jnp.dot(own_cols, own_part, preferred_element_type=jnp.float32)  2.79 us
    slice x1, local copies, waits for them, and re-layouts, shards(): current = combine(current, partner, blocks[3], tgt_place & 1, rank_rows)  2.77 us
  transfers between devices with their start and end apart: 4, of which 3 were waited for; matrix products, arithmetic and copies ran while one was open for 6% of the time, Pallas kernels for 0%

commit v1 on v0

v1 whole, which is shorter than its diff:
```python
import functools

import jax
import jax.numpy as jnp
from jax import lax
from jax.experimental import pallas as pl
from jax.experimental.pallas import tpu as pltpu
from jax.sharding import PartitionSpec as P

LANES = 128
RUNS = 4
GROUPS = 2
VMEM_MIB = 53
MODES = ("yy", "zz", "zz", "zz")
DEPTH = 2
ORDER = (
    "A0", "A1", "A2", "A3", "B0", "S0", "B1", "Z", "S1", "B2", "S2", "B3", "S3",
    "C10", "Y0", "C20", "C11", "C30", "C21", "D1", "C31", "D0", "E1", "D2", "E0", "D3", "E2", "E3",
)


def kernel(shape, coef, blocks, out, s0, s1, t1, v, w, r, s3, bv,
           load_sem, block_sem, send0, recv0, send1, recv1,
           send_y, recv_y, send_z, recv_z, send3, recv3, near_sem, far_sem):
    n_src, n_tgt, rank, chunks = shape
    nz = n_tgt // RUNS
    slab = rank // n_tgt
    in_group = nz // GROUPS
    src_top = n_src.bit_length() - 2
    src, tgt = lax.axis_index("src"), lax.axis_index("tgt")
    core = lax.rem(src, 2)
    jy, jz = tgt // nz, lax.rem(tgt, nz)
    up0 = pl.multiple_of(core * rank, rank)
    up1 = pl.multiple_of(lax.rem(src // (1 << src_top), 2) * rank, rank)
    up3 = pl.multiple_of(lax.rem(tgt, 2) * rank, rank)
    par = lax.rem(jy, 2)

    def flip(i, bit):
        return i + (1 << bit) * (1 - 2 * lax.rem(i // (1 << bit), 2))

    def y_place(d):
        return lax.rem(jy + d, RUNS) * nz + jz

    def z_place(d):
        return jy * nz + lax.rem(jz + d, nz)

    def signal(sem, peer_src, peer_tgt):
        pl.semaphore_signal(sem, inc=1, device_id={"src": peer_src, "tgt": peer_tgt},
                            device_id_type=pl.DeviceIdType.MESH)

    core_src, x_src = flip(src, 0), flip(src, src_top)

    barrier = pltpu.get_barrier_semaphore()
    signal(barrier, x_src - core, tgt)

    @pl.when(core == 1)
    def _():
        signal(barrier, core_src, tgt)

    for d in range(1, RUNS):
        signal(barrier, src - core, y_place(d))
    for d in range(1, nz):
        signal(barrier, src - core + 1, z_place(d))

    loads = []
    for c in range(chunks):
        loads.append(pltpu.make_async_copy(
            coef.at[0, 0, :, pl.ds(c * LANES, LANES)], s0.at[c, pl.ds(up0, rank)], load_sem.at[c]))
        loads[-1].start()
    block_loads = []
    for level in range(4):
        block_loads.append(pltpu.make_async_copy(blocks.at[level, 0, 0], bv.at[level], block_sem.at[level]))
        block_loads[-1].start()

    @pl.when(core == 0)
    def _():
        pl.semaphore_wait(barrier, 3 + 2 * (RUNS - 1))
        signal(near_sem, core_src, tgt)

    @pl.when(core == 1)
    def _():
        pl.semaphore_wait(near_sem, 1)

    def meet_far():
        @pl.when(core == 1)
        def _():
            pl.semaphore_wait(barrier, 2 * (nz - 1))
            signal(far_sem, core_src, tgt)

        @pl.when(core == 0)
        def _():
            pl.semaphore_wait(far_sem, 1)

    def remote(source, target, send, recv, peer_src, peer_tgt):
        return pltpu.make_async_remote_copy(
            src_ref=source, dst_ref=target, send_sem=send, recv_sem=recv,
            device_id={"src": peer_src, "tgt": peer_tgt}, device_id_type=pl.DeviceIdType.MESH)

    def same(buf, c, offset, send, recv, peer_src, peer_tgt):
        ref = buf.at[c, pl.ds(offset, rank)]
        return remote(ref, ref, send.at[c], recv.at[c], peer_src, peer_tgt)

    copies0 = [same(s0, c, up0, send0, recv0, core_src, tgt) for c in range(chunks)]
    copies1 = [same(s1, c, up1, send1, recv1, x_src, tgt) for c in range(chunks)]
    copies3 = [same(s3, c, up3, send3, recv3, src, flip(tgt, 0)) for c in range(chunks)]

    mine = jz // in_group

    def modes(c, way):
        return [g for g in range(GROUPS) if MODES[c][g] == way]

    def among(c, way):
        groups = modes(c, way)
        if len(groups) == GROUPS:
            return lambda f: f()
        if not groups:
            return lambda f: None
        return pl.when(mine == groups[0])

    def members(g):
        return pl.ds(g * in_group, in_group)

    def y_first(c):
        return [remote(t1.at[c, :, lax.rem(par + d, 2)], v.at[c, :, jy], send_y.at[c, mine, d - 1],
                       recv_y.at[c, mine, d - 1], src, y_place(d)) for d in (2, 1, 3)]

    def y_second(c, g):
        return [remote(w.at[c, lax.rem(par + d, 2), members(g)], r.at[c, jy, members(g)],
                       send_y.at[c, g, d - 1], recv_y.at[c, g, d - 1], src, y_place(d)) for d in (2, 1, 3)]

    def z_copies(c, first):
        copies = []
        for d in sorted(range(1, nz), key=lambda d: -min(d, nz - d)):
            there = lax.rem(jz + d, nz)
            source, target = (t1, w) if first else (v, r)
            source, target = source.at[c, there], target.at[c, :, jz]
            copies.append(remote(source, target, send_z.at[c, d - 1], recv_z.at[c, jz], src, z_place(d)))
        return copies

    def wait_z(c, g):
        for z in range(g * in_group, (g + 1) * in_group):
            buf = r if MODES[c][g] == "y" else w
            target = buf.at[c, :, z]

            @pl.when(jz != z)
            def _():
                remote(target, target, send_z.at[c, 0], recv_z.at[c, z], src, z_place(1)).wait_recv()

    def apply(level, stack):
        return jnp.dot(bv[level], stack, preferred_element_type=jnp.float32).astype(jnp.bfloat16)

    for c in range(chunks):
        loads[c].wait()
        copies0[c].start()

    under_way = []

    def finish_y(most):
        while len(under_way) > most:
            under_way.pop(0)()

    def wait_y_first(c):
        @among(c, "y")
        def _():
            for copy in y_first(c):
                copy.wait_send()

    def wait_y_second(c, g):
        for copy in y_second(c, g):
            copy.wait_send()

    for at, step in enumerate(ORDER):
        if step == "Z":
            meet_far()
            continue
        kind, c = step[0], int(step[1])
        if c >= chunks:
            continue
        if kind == "A":
            if c == 0:
                block_loads[0].wait()
            copies0[c].wait_recv()
            s1[c, pl.ds(up1, rank)] = apply(0, s0[c])
            copies1[c].start()
        elif kind == "B":
            if c == 0:
                block_loads[1].wait()
            copies1[c].wait_recv()
            second = apply(1, s1[c]).reshape(2, 2, nz, slab, LANES)
            for half in range(2):
                for p in range(2):
                    t1[c, :, p, half] = second[half, p]
        elif kind == "S":
            if modes(c, "y"):
                finish_y(DEPTH - 1)
                under_way.append(functools.partial(wait_y_first, c))

            @among(c, "y")
            def _():
                for copy in y_first(c):
                    copy.start()
                v[c, :, jy] = t1[c, :, par]

            @among(c, "z")
            def _():
                for copy in z_copies(c, True):
                    copy.start()
                w[c, :, jz] = t1[c, jz]
        elif kind == "Y":
            @among(c, "y")
            def _():
                for copy in y_first(c):
                    copy.wait_recv()
                for copy in z_copies(c, False):
                    copy.start()
                r[c, :, jz] = v[c, jz]
        elif kind == "C":
            g = int(step[2])
            wait_z(c, g)
            finish_y(DEPTH - 1)
            under_way.append(functools.partial(wait_y_second, c, g))
            for copy in y_second(c, g):
                copy.start()
            r[c, jy, members(g)] = w[c, par, members(g)]
        elif kind == "D":
            if not any(e[0] == "D" for e in ORDER[:at]):
                block_loads[2].wait()
            for g in range(GROUPS):
                if MODES[c][g] == "y":
                    wait_z(c, g)
                else:
                    for copy in y_second(c, g):
                        copy.wait_recv()
            stack = [r[c, :, :, half].reshape(rank, LANES) for half in range(2)]
            s3[c, pl.ds(up3, rank)] = apply(2, jnp.concatenate(stack, axis=0))
            copies3[c].start()
        else:
            if not any(e[0] == "E" for e in ORDER[:at]):
                block_loads[3].wait()
            copies3[c].wait_recv()
            out[0, 0, :, pl.ds(c * LANES, LANES)] = apply(3, s3[c])

    finish_y(0)
    for c in range(chunks):
        for copy in [copies0[c], copies1[c], copies3[c]]:
            copy.wait_send()

        @among(c, "y")
        def _():
            for copy in z_copies(c, False):
                copy.wait_send()

        @among(c, "z")
        def _():
            for copy in z_copies(c, True):
                copy.wait_send()


def shards(coefficients, transfer_blocks):
    rank, columns = coefficients.shape[2:]
    chunks = columns // LANES
    n_src, n_tgt = lax.axis_size("src"), lax.axis_size("tgt")
    slab = rank // n_tgt
    nz = n_tgt // RUNS
    kind = jnp.bfloat16
    dma = pltpu.SemaphoreType.DMA
    return pl.pallas_call(
        functools.partial(kernel, (n_src, n_tgt, rank, chunks)),
        out_shape=jax.ShapeDtypeStruct(coefficients.shape, kind),
        in_specs=[pl.BlockSpec(memory_space=pltpu.HBM)] * 2,
        out_specs=pl.BlockSpec(memory_space=pltpu.VMEM),
        scratch_shapes=[
            pltpu.VMEM((chunks, 2 * rank, LANES), kind),
            pltpu.VMEM((chunks, 2 * rank, LANES), kind),
            pltpu.VMEM((chunks, nz, 2, 2, slab, LANES), kind),
            pltpu.VMEM((chunks, nz, RUNS, 2, slab, LANES), kind),
            pltpu.VMEM((chunks, 2, nz, 2, slab, LANES), kind),
            pltpu.VMEM((chunks, RUNS, nz, 2, slab, LANES), kind),
            pltpu.VMEM((chunks, 2 * rank, LANES), kind),
            pltpu.VMEM((4, rank, 2 * rank), kind),
            dma((chunks,)), dma((4,)),
            dma((chunks,)), dma((chunks,)), dma((chunks,)), dma((chunks,)),
            dma((chunks, GROUPS, RUNS - 1)), dma((chunks, GROUPS, RUNS - 1)),
            dma((chunks, nz - 1)), dma((chunks, nz)),
            dma((chunks,)), dma((chunks,)),
            pltpu.SemaphoreType.REGULAR, pltpu.SemaphoreType.REGULAR,
        ],
        compiler_params=pltpu.CompilerParams(
            collective_id=0, has_side_effects=True, vmem_limit_bytes=VMEM_MIB * 2**20),
        cost_estimate=pl.CostEstimate(
            flops=4 * 2 * rank * 2 * rank * columns, bytes_accessed=6 * 2**20, transcendentals=0),
    )(coefficients, transfer_blocks)


def solution(mesh):
    return jax.shard_map(
        shards,
        mesh=mesh,
        in_specs=(P("src", "tgt", None, None), P(None, "src", "tgt", None, None)),
        out_specs=P("src", "tgt", None, None),
        check_vma=False,
    )
```

time: 86.7 us -> 54.7 us (0.63)
  Pallas kernels: 0 us -> 53.8 us
  waiting for transfers between devices: 50.6 us -> 0 us
  starting transfers between devices: 23.2 us -> 0 us
  matrix products: 8.38 us -> 0 us
  local copies, waits for them, and re-layouts: 2.89 us -> 0.8 us
  other arithmetic: 1.06 us -> 0 us
    pallas_call x0 -> x1, Pallas kernels: none -> 53.8 us  [shards(): pl.pallas_call(functools.partial(kernel, (n_src, n_tgt, rank, chunks)), o...]
    all_to_all x1 -> x0, waiting for transfers between devices: 27.2 us -> none  [shards(): lax.all_to_all(joined, 'tgt', split_axis=0, concat_axis=0, tiled=True)]
    ppermute x3 -> x0, waiting for transfers between devices: 23.4 us -> none  [from_partner(): lax.ppermute(value, axis, [(i, i ^ 1 << distance) for i in range(lax.axis...]
    all_to_all x1 -> x0, starting transfers between devices: 13.8 us -> none  [shards(): lax.all_to_all(joined, 'tgt', split_axis=0, concat_axis=0, tiled=True)]
    ppermute x3 -> x0, starting transfers between devices: 9.34 us -> none  [from_partner(): lax.ppermute(value, axis, [(i, i ^ 1 << distance) for i in range(lax.axis...]
    dot_general x8 -> x0, matrix products: 8.38 us -> none  [the longest x4 5.59 us: combine(): jnp.dot(other_cols, partner, preferred_element_type=jnp.float32)]
    slice x2 -> x0, local copies, waits for them, and re-layouts: 2.85 us -> none  [the longest x1 2.77 us: shards(): current = combine(current, partner, blocks[3], tgt_place & 1, rank_rows)]
    another operation x1 -> x0, other arithmetic: 1.06 us -> none  [shards(): joined = jnp.stack([pieces, mirrored], 1).reshape(2 * rank_rows, columns)]
  transfers between devices with their start and end apart: 4 -> 0, of which waited for: 3 -> 0; matrix products, arithmetic and copies ran while one was open for 6% -> 0% of each run, Pallas kernels for 0% -> 0%
where the time goes in v1:
time: 54.7 us; the launch traced here: 54.6 us
  Pallas kernels  53.8 us (98%)
  local copies, waits for them, and re-layouts  0.8 us (1%)
    pallas_call x1, Pallas kernels, shards(): pl.pallas_call(functools.partial(kernel, (n_src, n_tgt, rank, chunks)), o...  53.8 us

profile of v1, /device:TPU:16, one launch (start us, length us, event | category | flops | bytes accessed | tf_op | source)
XLA Modules:
  0.0 54.6 jit_solution(292225251272115075)
XLA Ops:
  0.0 53.8 %shard_map.28 = bf16[1,1,512,512]{3,2,1,0:T(8,128)(2,1)S(1)} custom-call(bf16[1,1,512,512]{3,2,1,0:T(8,128)(2,1)} %coef.1, bf16[4,1,1,512,1024]{4,3,2,1,0:T(8,128)(2,1)} %blocks.1), custom_call_target="tpu_custom_call" | custom-call | flops 2147483648 | bytes 6291456 | tf_op jit(solution)/shard_map/pallas_call | solution.py:267
  53.8 0.8 %copy.4 = bf16[1,1,512,512]{3,2,1,0:T(8,128)(2,1)} copy(bf16[1,1,512,512]{3,2,1,0:T(8,128)(2,1)S(1)} %shard_map.28) | data formatting | bytes 1048576

commit v2 on v1

--- a/solution.py
+++ b/solution.py
@@ -9,13 +9,14 @@
 
 LANES = 128
 RUNS = 4
-GROUPS = 2
+GROUPS = 4
 VMEM_MIB = 53
-MODES = ("yy", "zz", "zz", "zz")
-DEPTH = 2
+MODES = ("yyzz", "zzzz", "zzzz", "zzzz")
+DEPTH = 4
+PIECES = 2
 ORDER = (
-    "A0", "A1", "A2", "A3", "B0", "S0", "B1", "Z", "S1", "B2", "S2", "B3", "S3",
-    "C10", "Y0", "C20", "C11", "C30", "C21", "D1", "C31", "D0", "E1", "D2", "E0", "D3", "E2", "E3",
+    "A0", "A1", "A2", "A3", "B0", "Z1", "S0", "B1", "Z0", "S1", "B2", "S2", "C10", "C11", "B3", "S3", "Y0", "C20", "C21",
+    "C02", "C03", "C12", "C13", "D0", "C22", "C23", "C30", "C31", "D1", "C32", "C33", "D2", "E0", "D3", "E1", "E2", "E3",
 )
 
 
@@ -96,11 +97,17 @@
             src_ref=source, dst_ref=target, send_sem=send, recv_sem=recv,
             device_id={"src": peer_src, "tgt": peer_tgt}, device_id_type=pl.DeviceIdType.MESH)
 
+    piece = rank // PIECES
+
     def same(buf, c, offset, send, recv, peer_src, peer_tgt):
-        ref = buf.at[c, pl.ds(offset, rank)]
-        return remote(ref, ref, send.at[c], recv.at[c], peer_src, peer_tgt)
-
-    copies0 = [same(s0, c, up0, send0, recv0, core_src, tgt) for c in range(chunks)]
+        copies = []
+        for p in range(PIECES):
+            ref = buf.at[c, pl.ds(pl.multiple_of(offset + p * piece, piece), piece)]
+            copies.append(remote(ref, ref, send.at[c, p], recv.at[c, p], peer_src, peer_tgt))
+        return copies
+
+    copies0 = [remote(s0.at[c, pl.ds(up0, rank)], s0.at[c, pl.ds(up0, rank)], send0.at[c], recv0.at[c], core_src, tgt)
+               for c in range(chunks)]
     copies1 = [same(s1, c, up1, send1, recv1, x_src, tgt) for c in range(chunks)]
     copies3 = [same(s3, c, up3, send3, recv3, src, flip(tgt, 0)) for c in range(chunks)]
 
@@ -115,7 +122,7 @@
             return lambda f: f()
         if not groups:
             return lambda f: None
-        return pl.when(mine == groups[0])
+        return pl.when(functools.reduce(jnp.logical_or, [mine == g for g in groups]))
 
     def members(g):
         return pl.ds(g * in_group, in_group)
@@ -128,14 +135,14 @@
         return [remote(w.at[c, lax.rem(par + d, 2), members(g)], r.at[c, jy, members(g)],
                        send_y.at[c, g, d - 1], recv_y.at[c, g, d - 1], src, y_place(d)) for d in (2, 1, 3)]
 
-    def z_copies(c, first):
-        copies = []
-        for d in sorted(range(1, nz), key=lambda d: -min(d, nz - d)):
-            there = lax.rem(jz + d, nz)
+    def each_z(c, first, act):
+        for z in range(nz):
             source, target = (t1, w) if first else (v, r)
-            source, target = source.at[c, there], target.at[c, :, jz]
-            copies.append(remote(source, target, send_z.at[c, d - 1], recv_z.at[c, jz], src, z_place(d)))
-        return copies
+            source, target = source.at[c, z], target.at[c, :, jz]
+
+            @pl.when(jz != z)
+            def _():
+                act(remote(source, target, send_z.at[c, z], recv_z.at[c, jz], src, jy * nz + z))
 
     def wait_z(c, g):
         for z in range(g * in_group, (g + 1) * in_group):
@@ -144,10 +151,20 @@
 
             @pl.when(jz != z)
             def _():
-                remote(target, target, send_z.at[c, 0], recv_z.at[c, z], src, z_place(1)).wait_recv()
-
-    def apply(level, stack):
-        return jnp.dot(bv[level], stack, preferred_element_type=jnp.float32).astype(jnp.bfloat16)
+                remote(target, target, send_z.at[c, z], recv_z.at[c, z], src, jy * nz + z).wait_recv()
+
+    def dot(a, b):
+        return jnp.dot(a, b, preferred_element_type=jnp.float32)
+
+    def receive(level, buf, c, arrivals):
+        for copy in arrivals:
+            copy.wait_recv()
+        return dot(bv[level], buf[c]).astype(jnp.bfloat16)
+
+    def send_pieces(buf, c, offset, copies, make):
+        for p, copy in enumerate(copies):
+            buf[c, pl.ds(pl.multiple_of(offset + p * piece, piece), piece)] = make(p * piece)
+            copy.start()
 
     for c in range(chunks):
         loads[c].wait()
@@ -170,8 +187,8 @@
             copy.wait_send()
 
     for at, step in enumerate(ORDER):
-        if step == "Z":
-            meet_far()
+        if step[0] == "Z":
+            pl.when(mine // (GROUPS // 2) == int(step[1]))(meet_far)
             continue
         kind, c = step[0], int(step[1])
         if c >= chunks:
@@ -179,14 +196,12 @@
         if kind == "A":
             if c == 0:
                 block_loads[0].wait()
-            copies0[c].wait_recv()
-            s1[c, pl.ds(up1, rank)] = apply(0, s0[c])
-            copies1[c].start()
+            first = receive(0, s0, c, [copies0[c]])
+            send_pieces(s1, c, up1, copies1[c], lambda row: first[row:row + piece])
         elif kind == "B":
             if c == 0:
                 block_loads[1].wait()
-            copies1[c].wait_recv()
-            second = apply(1, s1[c]).reshape(2, 2, nz, slab, LANES)
+            second = receive(1, s1, c, copies1[c]).reshape(2, 2, nz, slab, LANES)
             for half in range(2):
                 for p in range(2):
                     t1[c, :, p, half] = second[half, p]
@@ -203,16 +218,14 @@
 
             @among(c, "z")
             def _():
-                for copy in z_copies(c, True):
-                    copy.start()
+                each_z(c, True, lambda copy: copy.start())
                 w[c, :, jz] = t1[c, jz]
         elif kind == "Y":
             @among(c, "y")
             def _():
                 for copy in y_first(c):
                     copy.wait_recv()
-                for copy in z_copies(c, False):
-                    copy.start()
+                each_z(c, False, lambda copy: copy.start())
                 r[c, :, jz] = v[c, jz]
         elif kind == "C":
             g = int(step[2])
@@ -232,28 +245,26 @@
                     for copy in y_second(c, g):
                         copy.wait_recv()
             stack = [r[c, :, :, half].reshape(rank, LANES) for half in range(2)]
-            s3[c, pl.ds(up3, rank)] = apply(2, jnp.concatenate(stack, axis=0))
-            copies3[c].start()
+            stack = jnp.concatenate(stack, axis=0)
+            send_pieces(s3, c, up3, copies3[c],
+                        lambda row: dot(bv[2, row:row + piece], stack).astype(jnp.bfloat16))
         else:
             if not any(e[0] == "E" for e in ORDER[:at]):
                 block_loads[3].wait()
-            copies3[c].wait_recv()
-            out[0, 0, :, pl.ds(c * LANES, LANES)] = apply(3, s3[c])
+            out[0, 0, :, pl.ds(c * LANES, LANES)] = receive(3, s3, c, copies3[c])
 
     finish_y(0)
     for c in range(chunks):
-        for copy in [copies0[c], copies1[c], copies3[c]]:
+        for copy in [copies0[c]] + copies1[c] + copies3[c]:
             copy.wait_send()
 
         @among(c, "y")
         def _():
-            for copy in z_copies(c, False):
-                copy.wait_send()
+            each_z(c, False, lambda copy: copy.wait_send())
 
         @among(c, "z")
         def _():
-            for copy in z_copies(c, True):
-                copy.wait_send()
+            each_z(c, True, lambda copy: copy.wait_send())
 
 
 def shards(coefficients, transfer_blocks):
@@ -279,10 +290,10 @@
             pltpu.VMEM((chunks, 2 * rank, LANES), kind),
             pltpu.VMEM((4, rank, 2 * rank), kind),
             dma((chunks,)), dma((4,)),
-            dma((chunks,)), dma((chunks,)), dma((chunks,)), dma((chunks,)),
+            dma((chunks,)), dma((chunks,)), dma((chunks, PIECES)), dma((chunks, PIECES)),
             dma((chunks, GROUPS, RUNS - 1)), dma((chunks, GROUPS, RUNS - 1)),
-            dma((chunks, nz - 1)), dma((chunks, nz)),
-            dma((chunks,)), dma((chunks,)),
+            dma((chunks, nz)), dma((chunks, nz)),
+            dma((chunks, PIECES)), dma((chunks, PIECES)),
             pltpu.SemaphoreType.REGULAR, pltpu.SemaphoreType.REGULAR,
         ],
         compiler_params=pltpu.CompilerParams(

time: 54.7 us -> 51 us (0.932)
  the two profiles are of different devices: /device:TPU:16 before, /device:TPU:2 now
where the time goes in v2:
time: 51 us; the launch traced here: 50.9 us
  Pallas kernels  50.1 us (98%)
  local copies, waits for them, and re-layouts  0.8 us (2%)
    pallas_call x1, Pallas kernels, shards(): pl.pallas_call(functools.partial(kernel, (n_src, n_tgt, rank, chunks)), o...  50.1 us

profile of v2, /device:TPU:2, one launch (start us, length us, event | category | flops | bytes accessed | tf_op | source)
XLA Modules:
  0.0 50.9 jit_solution(14742517008937929621)
XLA Ops:
  0.0 50.1 %shard_map.28 = bf16[1,1,512,512]{3,2,1,0:T(8,128)(2,1)S(1)} custom-call(bf16[1,1,512,512]{3,2,1,0:T(8,128)(2,1)} %coef.1, bf16[4,1,1,512,1024]{4,3,2,1,0:T(8,128)(2,1)} %blocks.1), custom_call_target="tpu_custom_call" | custom-call | flops 2147483648 | bytes 6291456 | tf_op jit(solution)/shard_map/pallas_call | solution.py:278
  50.1 0.8 %copy.4 = bf16[1,1,512,512]{3,2,1,0:T(8,128)(2,1)} copy(bf16[1,1,512,512]{3,2,1,0:T(8,128)(2,1)S(1)} %shard_map.28) | data formatting | bytes 1048576
